TPU v7x, 128 devices: a whole 4x4x4 slice. The times are simulated.
128 devices in a mesh: dp: 4 (over z), cp: 32 (over y, x, core).
Axes of the slice: x: 4, y: 4, z: 4, core: 2. Of those that a mesh axis runs over, the one named last changes fastest.
Arguments:
- pre_q_nope: bfloat16 [8192, 8192], P('cp', 'dp'), may hold values from -3 to 3
- pre_q_rope: bfloat16 [8192, 4096], P('cp', 'dp'), may hold values from -8 to 8
- pre_latent: bfloat16 [8192, 512], P('cp'), may hold values from -6 to 6
- pre_rope: bfloat16 [8192, 64], P('cp'), may hold values from -8 to 8
- up_keys: bfloat16 [64, 128, 512], P('dp'), may hold values from -0.5 to 0.5
- up_values: bfloat16 [64, 512, 128], P('dp'), may hold values from -1.1953125 to 1.1953125
- new_lengths: int32 [8], replicated, may hold values from 1 to 32, as said below
- new_hosts: int32 [8], replicated, may hold values from 0 to 127, as said below
- req_pages: int32 [1024, 32], P(('dp', 'cp')), may hold values from 0 to 95, as said below
- req_len: int32 [1024], P(('dp', 'cp')), may hold values from 1 to 2048, as said below
- row_request: int32 [128, 8], P(('dp', 'cp')), may hold values from 0 to 7, each once within a row
- cache_latent: bfloat16 [524288, 512], P(('dp', 'cp')), may hold values from -6 to 6
- cache_rope: bfloat16 [524288, 64], P(('dp', 'cp')), may hold values from -6 to 6
- dec_q_nope: bfloat16 [3, 1024, 8192], P(None, ('dp', 'cp')), may hold values from -3 to 3
- dec_q_rope: bfloat16 [3, 1024, 4096], P(None, ('dp', 'cp')), may hold values from -8 to 8
- new_latent: bfloat16 [3, 1024, 512], P(None, ('dp', 'cp')), may hold values from -6 to 6
- new_rope: bfloat16 [3, 1024, 64], P(None, ('dp', 'cp')), may hold values from -8 to 8
Outputs:
- prefill_out: bfloat16 [8192, 8192], P('cp', 'dp')
- decode_out: bfloat16 [3, 1024, 8192], P(None, ('dp', 'cp'))
Inputs may be any that keep to these rules, and one draw needn't show every extreme that they name: `new_lengths`: pages of each new request, in the order of the prefill stream; they sum to 128, and one request has 32. `new_hosts`: the device, numbered dp index times the size of cp plus cp index, that hosts each new request; no two alike. `req_pages`: the 32 pool pages of each request slot of a device, in order; pool pages 64 and up hold what arrives for a new request: the first slot of a hosting device lists exactly them in order, and no other slot names them. `req_len`: the first slot of a hosting device has 64 times its new request's pages; the second slot of every device has 2048, the third 1. `row_request`: each device's decode rows name each of its request slots once.
All inputs are finite; a program needn't handle non-finite values.
Results may differ from a plain program's by a relative error of at most 0.015.
Values may be sent and summed in bfloat16 or wider, within the bound.
A program may use at most 192 MiB of HBM per device.

v0:
```python
import jax
import jax.numpy as jnp
from jax import lax
from jax.sharding import PartitionSpec as P

DN = 128
DR = 64
DL = 512
DV = 128
PAGE = 64


NEGATIVE = -1e30


def from_behind(value, axis, steps):
    count = lax.axis_size(axis)
    first, last = (max(0, -steps), min(count, count - steps))
    return lax.ppermute(value, axis, [(source, source + steps) for source in range(first, last)])


def request_of(lengths, offset, count):
    starts = (jnp.cumsum(lengths) - lengths) * PAGE
    places = offset + jnp.arange(count, dtype=jnp.int32)
    return jnp.sum((places[:, None] >= starts[None, :]).astype(jnp.int32), axis=1) - 1


def masked_softmax(scores, allowed):
    scores = jnp.where(allowed, scores, NEGATIVE)
    summit = jnp.max(scores, axis=-1, keepdims=True)
    raised = jnp.where(allowed, jnp.exp(scores - summit), 0.0)
    return (raised / jnp.sum(raised, axis=-1, keepdims=True)).astype(jnp.bfloat16)


def decode_attend(queries, query_rope, keys_latent, keys_rope, usable, fresh_latent, fresh_rope):
    scaling = (DN + DR) ** (-0.5)
    step_count = queries.shape[0]
    cached = (
        jnp.einsum("srhl,rkl->srhk", queries, keys_latent, preferred_element_type=jnp.float32)
        + jnp.einsum("srhe,rke->srhk", query_rope, keys_rope, preferred_element_type=jnp.float32)
    ) * scaling
    recent = (
        jnp.einsum("srhl,trl->srht", queries, fresh_latent, preferred_element_type=jnp.float32)
        + jnp.einsum("srhe,tre->srht", query_rope, fresh_rope, preferred_element_type=jnp.float32)
    ) * scaling
    cache_mask = usable[None, :, None, :]
    steps_seen = jnp.arange(step_count, dtype=jnp.int32)
    recent_mask = (steps_seen[None, :] <= steps_seen[:, None])[:, None, None, :]
    cached = jnp.where(cache_mask, cached, NEGATIVE)
    recent = jnp.where(recent_mask, recent, NEGATIVE)
    summit = jnp.maximum(
        jnp.max(cached, axis=-1, keepdims=True), jnp.max(recent, axis=-1, keepdims=True)
    )
    cached_exp = jnp.where(cache_mask, jnp.exp(cached - summit), 0.0)
    recent_exp = jnp.where(recent_mask, jnp.exp(recent - summit), 0.0)
    denominator = jnp.sum(cached_exp, axis=-1, keepdims=True) + jnp.sum(
        recent_exp, axis=-1, keepdims=True
    )
    cached_weights = (cached_exp / denominator).astype(jnp.bfloat16)
    recent_weights = (recent_exp / denominator).astype(jnp.bfloat16)
    gathered = jnp.einsum(
        "srhk,rkl->srhl", cached_weights, keys_latent, preferred_element_type=jnp.float32
    ) + jnp.einsum(
        "srht,trl->srhl", recent_weights, fresh_latent, preferred_element_type=jnp.float32
    )
    return gathered.astype(jnp.bfloat16)


def on_device(
    pre_q_nope,
    pre_q_rope,
    pre_latent,
    pre_rope,
    up_keys,
    up_values,
    new_lengths,
    new_hosts,
    req_pages,
    req_len,
    row_request,
    cache_latent,
    cache_rope,
    dec_q_nope,
    dec_q_rope,
    new_latent,
    new_rope,
):
    token_rows = pre_latent.shape[0]
    heads_here = up_keys.shape[0]
    context_index = lax.axis_index("cp")
    scaling = (DN + DR) ** (-0.5)
    request_span = token_rows * lax.axis_size("cp") // 4
    reach_devices = (request_span + token_rows - 2) // token_rows
    window_rows = (reach_devices + 1) * token_rows
    joined = jnp.concatenate([pre_latent, pre_rope], axis=1)
    group_joined = lax.all_gather(joined, "cp", axis=0, tiled=True)
    earlier = []
    for distance in range(reach_devices, 0, -1):
        earlier.append(from_behind(joined, "cp", distance))
    window = jnp.concatenate(earlier + [joined], axis=0)
    window_latent = window[:, :DL]
    window_rope = window[:, DL:]
    queries = jnp.einsum(
        "thd,hdl->thl",
        pre_q_nope.reshape(token_rows, heads_here, DN),
        up_keys,
        preferred_element_type=jnp.float32,
    ).astype(jnp.bfloat16)
    rotary = pre_q_rope.reshape(token_rows, heads_here, DR)
    opening = context_index * token_rows
    owners = request_of(new_lengths, opening, token_rows)
    key_owners = request_of(new_lengths, opening - reach_devices * token_rows, window_rows)
    query_pos = jnp.arange(token_rows, dtype=jnp.int32)
    key_pos = jnp.arange(window_rows, dtype=jnp.int32) - reach_devices * token_rows
    allowed = (owners[:, None] == key_owners[None, :]) & (key_pos[None, :] <= query_pos[:, None])
    block_heads = 4
    group_count = heads_here // block_heads
    query_groups = jnp.transpose(
        queries.reshape(token_rows, group_count, block_heads, DL), (1, 0, 2, 3)
    )
    rotary_groups = jnp.transpose(
        rotary.reshape(token_rows, group_count, block_heads, DR), (1, 0, 2, 3)
    )
    value_groups = up_values.reshape(group_count, block_heads, DL, DV)

    def attend_group(packed):
        query_part, rotary_part, value_map = packed
        scores = (
            jnp.einsum("thl,jl->htj", query_part, window_latent, preferred_element_type=jnp.float32)
            + jnp.einsum(
                "thr,jr->htj", rotary_part, window_rope, preferred_element_type=jnp.float32
            )
        ) * scaling
        weights = masked_softmax(scores, allowed[None])
        latent_out = jnp.einsum(
            "htj,jl->thl", weights, window_latent, preferred_element_type=jnp.float32
        ).astype(jnp.bfloat16)
        return jnp.einsum(
            "thl,hlv->thv", latent_out, value_map, preferred_element_type=jnp.float32
        ).astype(jnp.bfloat16)

    group_outs = lax.map(attend_group, (query_groups, rotary_groups, value_groups))
    prefill_out = jnp.transpose(group_outs, (1, 0, 2, 3)).reshape(token_rows, heads_here * DV)
    device = lax.axis_index("dp") * lax.axis_size("cp") + context_index
    starts = jnp.cumsum(new_lengths) - new_lengths
    arrival = jnp.sum(jnp.where(new_hosts == device, starts, 0)) * PAGE
    padded_back = jnp.concatenate(
        [group_joined, jnp.zeros((request_span, DL + DR), jnp.bfloat16)], axis=0
    )
    arrived = lax.dynamic_slice_in_dim(padded_back, arrival, request_span, 0)
    pool_latent = jnp.concatenate([cache_latent, arrived[:, :DL]], axis=0)
    pool_rope = jnp.concatenate([cache_rope, arrived[:, DL:]], axis=0)
    slot_count = row_request.shape[1]
    step_count = dec_q_nope.shape[0]
    heads_all = dec_q_nope.shape[2] // DN
    rows_map = row_request.reshape(slot_count)
    picker = (rows_map[:, None] == jnp.arange(slot_count, dtype=jnp.int32)[None, :]).astype(
        jnp.int32
    )
    row_pages = jnp.sum(picker[:, :, None] * req_pages[None, :, :], axis=1)
    row_counts = jnp.sum(picker * req_len[None, :], axis=1)
    token_index = (
        row_pages[:, :, None] * PAGE + jnp.arange(PAGE, dtype=jnp.int32)[None, None, :]
    ).reshape(slot_count, request_span)
    keys_latent = pool_latent[token_index]
    keys_rope = pool_rope[token_index]
    usable = jnp.arange(request_span, dtype=jnp.int32)[None, :] < row_counts[:, None]
    every_key, every_value = (
        lax.all_gather(up_keys, "dp", axis=0, tiled=True),
        lax.all_gather(up_values, "dp", axis=0, tiled=True),
    )
    dec_queries = jnp.einsum(
        "srhd,hdl->srhl",
        dec_q_nope.reshape(step_count, slot_count, heads_all, DN),
        every_key,
        preferred_element_type=jnp.float32,
    ).astype(jnp.bfloat16)
    dec_rotary = dec_q_rope.reshape(step_count, slot_count, heads_all, DR)
    decode_latent = decode_attend(
        dec_queries, dec_rotary, keys_latent, keys_rope, usable, new_latent, new_rope
    )
    decode_out = jnp.einsum(
        "srhl,hlv->srhv", decode_latent, every_value, preferred_element_type=jnp.float32
    ).astype(jnp.bfloat16)
    decode_out = decode_out.reshape(step_count, slot_count, heads_all * DV)
    return (prefill_out, decode_out)


def solution(mesh):
    placed = (
        P("cp", "dp"),
        P("cp", "dp"),
        P("cp", None),
        P("cp", None),
        P("dp", None, None),
        P("dp", None, None),
        P(),
        P(),
        P(("dp", "cp"), None),
        P(("dp", "cp")),
        P(("dp", "cp"), None),
        P(("dp", "cp"), None),
        P(("dp", "cp"), None),
        P(None, ("dp", "cp"), None),
        P(None, ("dp", "cp"), None),
        P(None, ("dp", "cp"), None),
        P(None, ("dp", "cp"), None),
    )
    return jax.shard_map(
        on_device,
        mesh=mesh,
        in_specs=placed,
        out_specs=(P("cp", "dp"), P(None, ("dp", "cp"), None)),
        check_vma=False,
    )
```

profile of v0, /device:TPU:1, one launch (start us, length us, event | category | flops | bytes accessed | tf_op | source)
XLA Modules:
  0.0 362.7 jit_solution(14533081332850790467)
XLA Ops:
  10.9 4.8 %collective-permute-start = (bf16[256,576]{1,0:T(8,128)(2,1)}, bf16[256,576]{1,0:T(8,128)(2,1)}, u32[]{:S(2)}, u32[]{:S(2)}) collective-permute-start(bf16[256,576]{1,0:T(8,128)(2,1)} %pad_maximum_fusion.2), channel_id=1, source_target_pairs={{0,8},{1,9},{2,10},{3,11},{4,12},{5,13},{6,14},{7,15},{8,16},{9,17... | collective-permute-start | bytes 884744 | tf_op jit(solution)/shard_map/ppermute | solution.py:19
  15.7 4.0 %collective-permute-start.1 = (bf16[256,576]{1,0:T(8,128)(2,1)}, bf16[256,576]{1,0:T(8,128)(2,1)}, u32[]{:S(2)}, u32[]{:S(2)}) collective-permute-start(bf16[256,576]{1,0:T(8,128)(2,1)} %pad_maximum_fusion.2), channel_id=1, source_target_pairs={{0,7},{1,8},{2,9},{3,10},{4,11},{5,12},{6,13},{7,14},{8,15},{9,16}... | collective-permute-start | bytes 884744 | tf_op jit(solution)/shard_map/ppermute | solution.py:19
  19.7 4.4 %collective-permute-start.2 = (bf16[256,576]{1,0:T(8,128)(2,1)}, bf16[256,576]{1,0:T(8,128)(2,1)}, u32[]{:S(2)}, u32[]{:S(2)}) collective-permute-start(bf16[256,576]{1,0:T(8,128)(2,1)} %pad_maximum_fusion.2), channel_id=1, source_target_pairs={{0,6},{1,7},{2,8},{3,9},{4,10},{5,11},{6,12},{7,13},{8,14},{9,15},... | collective-permute-start | bytes 884744 | tf_op jit(solution)/shard_map/ppermute | solution.py:19
  27.0 4.4 %collective-permute-start.4 = (bf16[256,576]{1,0:T(8,128)(2,1)}, bf16[256,576]{1,0:T(8,128)(2,1)}, u32[]{:S(2)}, u32[]{:S(2)}) collective-permute-start(bf16[256,576]{1,0:T(8,128)(2,1)} %pad_maximum_fusion.2), channel_id=1, source_target_pairs={{0,4},{1,5},{2,6},{3,7},{4,8},{5,9},{6,10},{7,11},{8,12},{9,13},{1... | collective-permute-start | bytes 884744 | tf_op jit(solution)/shard_map/ppermute | solution.py:19
  38.2 3.2 convolution_convert_fusion
  41.8 4.0 %copy.74 = bf16[16,512,128]{1,2,0:T(8,128)(2,1)} copy(bf16[16,512,128]{2,1,0:T(8,128)(2,1)} %param.24) | data formatting | bytes 4194304 | tf_op args[5]
  47.7 7.4 %copy.77 = bf16[256,4,4,512]{3,0,2,1:T(8,128)(2,1)} copy(bf16[256,4,4,512]{0,3,2,1:T(8,128)(2,1)} %bitcast.186) | data formatting | bytes 8388608 | tf_op jit(solution)/shard_map/reshape | solution.py:119
  62.0 3.0 collective-permute-start.7
  68.1 3.5 collective-permute-done.6
  71.7 4.1 %collective-permute-done.7 = bf16[256,576]{1,0:T(8,128)(2,1)S(1)} collective-permute-done((bf16[256,576]{1,0:T(8,128)(2,1)S(1)}, bf16[256,576]{1,0:T(8,128)(2,1)S(1)}, u32[]{:S(2)}, u32[]{:S(2)}) %collective-permute-start.7) | collective-permute-done | bytes 294944 | tf_op jit(solution)/shard_map/ppermute | solution.py:19
  77.8 80.5 %while.11 = (s32[]{:T(128)}, bf16[4,256,4,128]{1,3,2,0:T(8,128)(2,1)S(1)}, bf16[4,4,512,128]{2,3,1,0:T(8,128)(2,1)}, bf16[4,256,4,512]{3,1,2,0:T(8,128)(2,1)}, b...) while((s32[]{:T(128)}, ...), condition=%wide.region_6.7_spmd.clone, body=%wide.region_3.6_spmd.clone.sunk | while | flops 5289347072 | bytes 65401456 | solution.py:142
  78.0 4.6 %fusion.122 = f32[256,4,2304]{2,0,1:T(8,128)S(1)} fusion(bf16[2304,512]{1,0:T(8,128)(2,1)} %get-tuple-element.231, bf16[4,256,4,512]{3,1,2,0:T(8,128)(2,1)} %get-tuple-element.230, s32[]{:T(128)} %get-tuple-element.216), kind=kOutput, calls=%fused_computation.13.clone.1 | convolution fusion | flops 2415919104 | bytes 12845568 | tf_op jit(solution)/shard_map/while/body/eval_jaxpr/thl,jl->htj/dot_general | solution.py:129
  85.3 5.0 %fusion.124 = (f32[4,256]{1,0:T(4,128)S(1)}, f32[4,256,2304]{2,1,0:T(8,128)}) fusion(f32[256,4,2304]{2,0,1:T(8,128)S(1)} %multiply_select_fusion.3, pred[256,2304]{1,0:T(8,128)(4,1)S(1)} %fusion.123), kind=kOutput, calls=%fused_computation.116.clone.1 | output fusion | flops 7080191 | bytes 19468288 | tf_op jit(solution)/shard_map/while/body/eval_jaxpr/sub | solution.py:31
  90.3 7.4 %fusion.125 = bf16[4,256,4,128]{1,3,2,0:T(8,128)(2,1)S(1)} fusion(bf16[4,256,4,128]{1,3,2,0:T(8,128)(2,1)S(1)} %get-tuple-element.217, s32[]{:T(128)} %get-tuple-element.216, bf16[2304,512]{1,0:T(8,128)(2,1)} %get-tuple-element.231, f32[4,256,2304]{2,1,0:T(8,128)} %get-tuple-element.203, f32[4,256]{1,0:T(4,128)S(1)} %get-tuple-element.204, ...), kind=kOutput, calls=%fused_computation.22.clone.1 | convolution fusion | flops 2555510784 | bytes 12588032 | tf_op jit(solution)/shard_map/while/body/eval_jaxpr/thl,hlv->thv/dot_general | solution.py:138
  97.8 4.6 %fusion.122 = f32[256,4,2304]{2,0,1:T(8,128)S(1)} fusion(bf16[2304,512]{1,0:T(8,128)(2,1)} %get-tuple-element.231, bf16[4,256,4,512]{3,1,2,0:T(8,128)(2,1)} %get-tuple-element.230, s32[]{:T(128)} %get-tuple-element.216), kind=kOutput, calls=%fused_computation.13.clone.1 | convolution fusion | flops 2415919104 | bytes 12845568 | tf_op jit(solution)/shard_map/while/body/eval_jaxpr/thl,jl->htj/dot_general | solution.py:129
  105.0 5.1 %fusion.124 = (f32[4,256]{1,0:T(4,128)S(1)}, f32[4,256,2304]{2,1,0:T(8,128)}) fusion(f32[256,4,2304]{2,0,1:T(8,128)S(1)} %multiply_select_fusion.3, pred[256,2304]{1,0:T(8,128)(4,1)S(1)} %fusion.123), kind=kOutput, calls=%fused_computation.116.clone.1 | output fusion | flops 7080191 | bytes 19468288 | tf_op jit(solution)/shard_map/while/body/eval_jaxpr/sub | solution.py:31
  110.2 7.5 %fusion.125 = bf16[4,256,4,128]{1,3,2,0:T(8,128)(2,1)S(1)} fusion(bf16[4,256,4,128]{1,3,2,0:T(8,128)(2,1)S(1)} %get-tuple-element.217, s32[]{:T(128)} %get-tuple-element.216, bf16[2304,512]{1,0:T(8,128)(2,1)} %get-tuple-element.231, f32[4,256,2304]{2,1,0:T(8,128)} %get-tuple-element.203, f32[4,256]{1,0:T(4,128)S(1)} %get-tuple-element.204, ...), kind=kOutput, calls=%fused_computation.22.clone.1 | convolution fusion | flops 2555510784 | bytes 12588032 | tf_op jit(solution)/shard_map/while/body/eval_jaxpr/thl,hlv->thv/dot_general | solution.py:138
  117.6 4.7 %fusion.122 = f32[256,4,2304]{2,0,1:T(8,128)S(1)} fusion(bf16[2304,512]{1,0:T(8,128)(2,1)} %get-tuple-element.231, bf16[4,256,4,512]{3,1,2,0:T(8,128)(2,1)} %get-tuple-element.230, s32[]{:T(128)} %get-tuple-element.216), kind=kOutput, calls=%fused_computation.13.clone.1 | convolution fusion | flops 2415919104 | bytes 12845568 | tf_op jit(solution)/shard_map/while/body/eval_jaxpr/thl,jl->htj/dot_general | solution.py:129
  124.9 5.0 %fusion.124 = (f32[4,256]{1,0:T(4,128)S(1)}, f32[4,256,2304]{2,1,0:T(8,128)}) fusion(f32[256,4,2304]{2,0,1:T(8,128)S(1)} %multiply_select_fusion.3, pred[256,2304]{1,0:T(8,128)(4,1)S(1)} %fusion.123), kind=kOutput, calls=%fused_computation.116.clone.1 | output fusion | flops 7080191 | bytes 19468288 | tf_op jit(solution)/shard_map/while/body/eval_jaxpr/sub | solution.py:31
  130.0 8.3 %fusion.125 = bf16[4,256,4,128]{1,3,2,0:T(8,128)(2,1)S(1)} fusion(bf16[4,256,4,128]{1,3,2,0:T(8,128)(2,1)S(1)} %get-tuple-element.217, s32[]{:T(128)} %get-tuple-element.216, bf16[2304,512]{1,0:T(8,128)(2,1)} %get-tuple-element.231, f32[4,256,2304]{2,1,0:T(8,128)} %get-tuple-element.203, f32[4,256]{1,0:T(4,128)S(1)} %get-tuple-element.204, ...), kind=kOutput, calls=%fused_computation.22.clone.1 | convolution fusion | flops 2555510784 | bytes 12588032 | tf_op jit(solution)/shard_map/while/body/eval_jaxpr/thl,hlv->thv/dot_general | solution.py:138
  138.3 4.7 %fusion.122 = f32[256,4,2304]{2,0,1:T(8,128)S(1)} fusion(bf16[2304,512]{1,0:T(8,128)(2,1)} %get-tuple-element.231, bf16[4,256,4,512]{3,1,2,0:T(8,128)(2,1)} %get-tuple-element.230, s32[]{:T(128)} %get-tuple-element.216), kind=kOutput, calls=%fused_computation.13.clone.1 | convolution fusion | flops 2415919104 | bytes 12845568 | tf_op jit(solution)/shard_map/while/body/eval_jaxpr/thl,jl->htj/dot_general | solution.py:129
  145.6 5.1 %fusion.124 = (f32[4,256]{1,0:T(4,128)S(1)}, f32[4,256,2304]{2,1,0:T(8,128)}) fusion(f32[256,4,2304]{2,0,1:T(8,128)S(1)} %multiply_select_fusion.3, pred[256,2304]{1,0:T(8,128)(4,1)S(1)} %fusion.123), kind=kOutput, calls=%fused_computation.116.clone.1 | output fusion | flops 7080191 | bytes 19468288 | tf_op jit(solution)/shard_map/while/body/eval_jaxpr/sub | solution.py:31
  150.7 7.6 %fusion.125 = bf16[4,256,4,128]{1,3,2,0:T(8,128)(2,1)S(1)} fusion(bf16[4,256,4,128]{1,3,2,0:T(8,128)(2,1)S(1)} %get-tuple-element.217, s32[]{:T(128)} %get-tuple-element.216, bf16[2304,512]{1,0:T(8,128)(2,1)} %get-tuple-element.231, f32[4,256,2304]{2,1,0:T(8,128)} %get-tuple-element.203, f32[4,256]{1,0:T(4,128)S(1)} %get-tuple-element.204, ...), kind=kOutput, calls=%fused_computation.22.clone.1 | convolution fusion | flops 2555510784 | bytes 12588032 | tf_op jit(solution)/shard_map/while/body/eval_jaxpr/thl,hlv->thv/dot_general | solution.py:138
  159.8 4.6 %fusion.50 = bf16[3,8,64,512]{3,1,0,2:T(8,128)(2,1)S(1)} fusion(bf16[64,128,512]{2,1,0:T(8,128)(2,1)} %all-gather.6.cloned.1.call-done, bf16[3,8,8192]{2,1,0:T(8,128)(2,1)S(1)} %copy-done.16), kind=kOutput, calls=%fused_computation.53 | convolution fusion | flops 202113024 | bytes 10354688
  170.0 3.1 pad_maximum_fusion
  173.1 71.0 %gather_fusion = bf16[16384,512]{1,0:T(8,128)(2,1)} fusion(bf16[6144,512]{1,0:T(8,128)(2,1)} %pad_maximum_fusion, s32[16384]{0:T(1024)S(1)} %copy-done.10), kind=kCustom, calls=%fused_computation | custom fusion | bytes 33619968 | tf_op jit(solution)/shard_map/gather | solution.py:165
  245.8 57.8 %gather_fusion.1 = bf16[16384,64]{1,0:T(8,128)(2,1)} fusion(bf16[6144,64]{1,0:T(8,128)(2,1)S(1)} %pad_maximum_fusion.1, s32[16384]{0:T(1024)S(1)} %copy-done.10), kind=kCustom, calls=%fused_computation.1 | custom fusion | bytes 4259840 | tf_op jit(solution)/shard_map/gather | solution.py:166
  303.6 12.6 %fusion.53 = f32[8,2048,3,64]{1,3,2,0:T(8,128)} fusion(bf16[8,2048,512,1]{2,1,3,0:T(8,128)(2,1)} %bitcast.184, bf16[3,8,64,512]{3,1,0,2:T(8,128)(2,1)} %copy-done.3), kind=kOutput, calls=%fused_computation.56 | convolution fusion | flops 3221225472 | bytes 30932992 | tf_op jit(solution)/shard_map/srhl,rkl->srhk/dot_general | solution.py:39
  316.2 12.9 %bitcast_reduce_fusion.1 = (f32[3,8,64]{2,0,1:T(4,128)S(1)}, f32[8,2048,3,64]{1,3,2,0:T(8,128)}) fusion(f32[8,2048,3,64]{1,3,2,0:T(8,128)} %fusion.53, bf16[8,2048,64,1]{2,1,3,0:T(8,128)(2,1)} %bitcast.187, bf16[3,8,64,64]{3,2,1,0:T(8,128)(2,1)S(1)} %copy-done.7, pred[8,2048]{1,0:T(8,128)(4,1)S(1)} %copy-done.17), kind=kOutput, calls=%fused_computation.36 | convolution fusion | flops 415234560 | bytes 27482112 | tf_op jit(solution)/shard_map/srhe,rke->srhk/dot_general | solution.py:40
  329.2 6.4 %fusion.43 = f32[3,8,64]{2,0,1:T(4,128)S(1)} fusion(f32[8,2048,3,64]{1,3,2,0:T(8,128)} %get-tuple-element.135, f32[3,8,64]{2,0,1:T(4,128)S(1)} %max.8, pred[8,2048]{1,0:T(8,128)(4,1)S(1)} %copy-done.17), kind=kLoop, calls=%fused_computation.41 | loop fusion | flops 9435648 | bytes 12611584 | tf_op jit(solution)/shard_map/reduce_sum | solution.py:56
  337.9 12.2 %fusion.48 = bf16[3,8,64,512]{3,2,0,1:T(8,128)(2,1)S(1)} fusion(f32[8,3,64,512]{3,2,1,0:T(8,128)} %fusion.85, bf16[8,2048,512,1]{2,1,3,0:T(8,128)(2,1)} %bitcast.185, f32[8,2048,3,64]{1,3,2,0:T(8,128)} %get-tuple-element.135, f32[3,8,64]{2,0,1:T(4,128)S(1)} %add.122, f32[3,8,64]{2,0,1:T(4,128)S(1)} %max.8, pred[8,2048]{1,0:T(8,128)(4,1)S(1)} %copy-done.17), kind=kOutput, calls=%fused_computation.48 | convolution fusion | flops 3235381248 | bytes 34107392 | tf_op jit(solution)/shard_map/srhk,rkl->srhl/dot_general | solution.py:61
  350.2 5.2 %fusion.60 = bf16[64,3,1,8,128]{4,3,2,1,0:T(8,128)(2,1)S(1)} fusion(bf16[64,512,128]{2,1,0:T(8,128)(2,1)} %all-gather.8.cloned.1.call-done, bf16[3,8,64,512]{3,2,0,1:T(8,128)(2,1)S(1)} %fusion.48), kind=kOutput, calls=%fused_computation.59 | convolution fusion | flops 201523200 | bytes 10354688 | tf_op jit(solution)/shard_map/srhl,hlv->srhv/dot_general | solution.py:182
  (122 shorter events, 49.2 us)
Async XLA Ops:
  7.2 31.0 %copy-start = (bf16[256,2048]{1,0:T(8,128)(2,1)S(1)}, bf16[256,2048]{1,0:T(8,128)(2,1)}, u32[]{:S(2)}) copy-start(bf16[256,2048]{1,0:T(8,128)(2,1)} %param.19) | copy-start | bytes 3145732
  7.2 31.0 %copy-start.2 = (bf16[16,128,512]{2,1,0:T(8,128)(2,1)S(1)}, bf16[16,128,512]{2,1,0:T(8,128)(2,1)}, u32[]{:S(2)}) copy-start(bf16[16,128,512]{2,1,0:T(8,128)(2,1)} %param.23) | copy-start | bytes 6291460
  7.2 24.2 %copy-start.21 = (s32[1,8]{1,0:T(1,128)S(1)}, s32[1,8]{1,0:T(1,128)}, u32[]{:S(2)}) copy-start(s32[1,8]{1,0:T(1,128)} %param.29) | copy-start | bytes 100
  7.2 24.3 %copy-start.20 = (s32[8,32]{1,0:T(8,128)S(1)}, s32[8,32]{1,0:T(8,128)}, u32[]{:S(2)}) copy-start(s32[8,32]{1,0:T(8,128)} %param.27) | copy-start | bytes 3076
  7.2 25.3 %copy-start.22 = (s32[8]{0:T(128)S(1)}, s32[8]{0:T(128)}, u32[]{:S(2)}) copy-start(s32[8]{0:T(128)} %param.28) | copy-start | bytes 100
  7.2 152.6 %all-gather.6.cloned.1.call-start = ((), (), s32[]{:S(2)}) async-start(), calls=%async_computation.1 | async-start | bytes 10485760 | tf_op jit(solution)/shard_map/all_gather | solution.py:169
  8.0 158.4 %all-gather.4.cloned.1.call-start = ((), (), s32[]{:S(2)}) async-start(), calls=%async_computation | async-start | bytes 10813440 | tf_op jit(solution)/shard_map/all_gather | solution.py:96
  9.0 23.7 %copy-start.11 = (bf16[256,64]{1,0:T(8,128)(2,1)}, bf16[256,64]{1,0:T(8,128)(2,1)S(1)}, u32[]{:S(2)}) copy-start(bf16[256,64]{1,0:T(8,128)(2,1)S(1)} %copy.78) | copy-start | bytes 98308
  10.8 339.4 %all-gather.8.cloned.1.call-start = ((), (), s32[]{:S(2)}) async-start(), calls=%async_computation.2 | async-start | bytes 10485760 | tf_op jit(solution)/shard_map/all_gather | solution.py:170
  10.9 44.5 %collective-permute-start = (bf16[256,576]{1,0:T(8,128)(2,1)}, bf16[256,576]{1,0:T(8,128)(2,1)}, u32[]{:S(2)}, u32[]{:S(2)}) collective-permute-start(bf16[256,576]{1,0:T(8,128)(2,1)} %pad_maximum_fusion.2), channel_id=1, source_target_pairs={{0,8},{1,9},{2,10},{3,11},{4,12},{5,13},{6,14},{7,15},{8,16},{9,17... | collective-permute-start | bytes 884744 | tf_op jit(solution)/shard_map/ppermute | solution.py:19
  15.7 43.2 %collective-permute-start.1 = (bf16[256,576]{1,0:T(8,128)(2,1)}, bf16[256,576]{1,0:T(8,128)(2,1)}, u32[]{:S(2)}, u32[]{:S(2)}) collective-permute-start(bf16[256,576]{1,0:T(8,128)(2,1)} %pad_maximum_fusion.2), channel_id=1, source_target_pairs={{0,7},{1,8},{2,9},{3,10},{4,11},{5,12},{6,13},{7,14},{8,15},{9,16}... | collective-permute-start | bytes 884744 | tf_op jit(solution)/shard_map/ppermute | solution.py:19
  19.7 42.3 %collective-permute-start.2 = (bf16[256,576]{1,0:T(8,128)(2,1)}, bf16[256,576]{1,0:T(8,128)(2,1)}, u32[]{:S(2)}, u32[]{:S(2)}) collective-permute-start(bf16[256,576]{1,0:T(8,128)(2,1)} %pad_maximum_fusion.2), channel_id=1, source_target_pairs={{0,6},{1,7},{2,8},{3,9},{4,10},{5,11},{6,12},{7,13},{8,14},{9,15},... | collective-permute-start | bytes 884744 | tf_op jit(solution)/shard_map/ppermute | solution.py:19
  24.1 41.9 %collective-permute-start.3 = (bf16[256,576]{1,0:T(8,128)(2,1)}, bf16[256,576]{1,0:T(8,128)(2,1)}, u32[]{:S(2)}, u32[]{:S(2)}) collective-permute-start(bf16[256,576]{1,0:T(8,128)(2,1)} %pad_maximum_fusion.2), channel_id=1, source_target_pairs={{0,5},{1,6},{2,7},{3,8},{4,9},{5,10},{6,11},{7,12},{8,13},{9,14},{... | collective-permute-start | bytes 884744 | tf_op jit(solution)/shard_map/ppermute | solution.py:19
  27.0 40.1 %collective-permute-start.4 = (bf16[256,576]{1,0:T(8,128)(2,1)}, bf16[256,576]{1,0:T(8,128)(2,1)}, u32[]{:S(2)}, u32[]{:S(2)}) collective-permute-start(bf16[256,576]{1,0:T(8,128)(2,1)} %pad_maximum_fusion.2), channel_id=1, source_target_pairs={{0,4},{1,5},{2,6},{3,7},{4,8},{5,9},{6,10},{7,11},{8,12},{9,13},{1... | collective-permute-start | bytes 884744 | tf_op jit(solution)/shard_map/ppermute | solution.py:19
  34.7 11.1 %copy-start.6 = (bf16[3,8,64,64]{3,2,1,0:T(8,128)(2,1)}, bf16[3,8,64,64]{3,2,1,0:T(8,128)(2,1)S(1)}, u32[]{:S(2)}) copy-start(bf16[3,8,64,64]{3,2,1,0:T(8,128)(2,1)S(1)} %reshape.202) | copy-start | bytes 589828
  36.1 5.3 %copy-start.19 = (bf16[3,8,64]{2,1,0:T(8,128)(2,1)S(1)}, bf16[3,8,64]{2,1,0:T(8,128)(2,1)}, u32[]{:S(2)}) copy-start(bf16[3,8,64]{2,1,0:T(8,128)(2,1)} %param.35) | copy-start | bytes 9220
  41.4 4.9 %copy-start.13 = (bf16[4096,64]{0,1:T(8,128)(2,1)S(1)}, bf16[4096,64]{0,1:T(8,128)(2,1)}, u32[]{:S(2)}) copy-start(bf16[4096,64]{0,1:T(8,128)(2,1)} %param.31) | copy-start | bytes 1572868
  47.7 7.4 %copy-start.14 = (bf16[256,1024]{1,0:T(8,128)(2,1)S(1)}, bf16[256,1024]{1,0:T(8,128)(2,1)}, u32[]{:S(2)}) copy-start(bf16[256,1024]{1,0:T(8,128)(2,1)} %param.20) | copy-start | bytes 1572868
  47.7 7.7 %copy-start.8 = (bf16[256,576]{1,0:T(8,128)(2,1)S(1)}, bf16[256,576]{1,0:T(8,128)(2,1)}, u32[]{:S(2)}) copy-start(bf16[256,576]{1,0:T(8,128)(2,1)} %pad_maximum_fusion.2) | copy-start | bytes 884740
  55.1 20.7 %copy-start.9 = (bf16[256,512]{1,0:T(8,128)(2,1)S(1)}, bf16[256,512]{1,0:T(8,128)(2,1)}, u32[]{:S(2)}) copy-start(bf16[256,512]{1,0:T(8,128)(2,1)} %param.21) | copy-start | bytes 786436
  55.1 20.8 %copy-start.12 = (bf16[256,64]{1,0:T(8,128)(2,1)S(1)}, bf16[256,64]{1,0:T(8,128)(2,1)}, u32[]{:S(2)}) copy-start(bf16[256,64]{1,0:T(8,128)(2,1)} %copy-done.11) | copy-start | bytes 98308
  55.4 12.7 %collective-permute-start.5 = (bf16[256,576]{1,0:T(8,128)(2,1)S(1)}, bf16[256,576]{1,0:T(8,128)(2,1)S(1)}, u32[]{:S(2)}, u32[]{:S(2)}) collective-permute-start(bf16[256,576]{1,0:T(8,128)(2,1)S(1)} %copy-done.8), channel_id=1, source_target_pairs={{0,3},{1,4},{2,5},{3,6},{4,7},{5,8},{6,9},{7,10},{8,11},{9,12},{10... | collective-permute-start | bytes 884744 | tf_op jit(solution)/shard_map/ppermute | solution.py:19
  58.8 12.8 %collective-permute-start.6 = (bf16[256,576]{1,0:T(8,128)(2,1)S(1)}, bf16[256,576]{1,0:T(8,128)(2,1)S(1)}, u32[]{:S(2)}, u32[]{:S(2)}) collective-permute-start(bf16[256,576]{1,0:T(8,128)(2,1)S(1)} %copy-done.8), channel_id=1, source_target_pairs={{0,2},{1,3},{2,4},{3,5},{4,6},{5,7},{6,8},{7,9},{8,10},{9,11},{10,... | collective-permute-start | bytes 884744 | tf_op jit(solution)/shard_map/ppermute | solution.py:19
  62.0 13.9 %collective-permute-start.7 = (bf16[256,576]{1,0:T(8,128)(2,1)S(1)}, bf16[256,576]{1,0:T(8,128)(2,1)S(1)}, u32[]{:S(2)}, u32[]{:S(2)}) collective-permute-start(bf16[256,576]{1,0:T(8,128)(2,1)S(1)} %copy-done.8), channel_id=1, source_target_pairs={{0,1},{1,2},{2,3},{3,4},{4,5},{5,6},{6,7},{7,8},{8,9},{9,10},{10,1... | collective-permute-start | bytes 884744 | tf_op jit(solution)/shard_map/ppermute | solution.py:19
  71.7 6.1 %copy-start.15 = (s32[2304]{0:T(1024)S(1)}, s32[2304]{0:T(1024)}, u32[]{:S(2)}) copy-start(s32[2304]{0:T(1024)} %get-tuple-element.212) | copy-start | bytes 27652
  77.8 82.0 %copy-start.16 = (bf16[3,8,8192]{2,1,0:T(8,128)(2,1)S(1)}, bf16[3,8,8192]{2,1,0:T(8,128)(2,1)}, u32[]{:S(2)}) copy-start(bf16[3,8,8192]{2,1,0:T(8,128)(2,1)} %param.32) | copy-start | bytes 1179652
  159.8 5.7 %copy-start.18 = (bf16[3,8,512]{2,1,0:T(8,128)(2,1)S(1)}, bf16[3,8,512]{2,1,0:T(8,128)(2,1)}, u32[]{:S(2)}) copy-start(bf16[3,8,512]{2,1,0:T(8,128)(2,1)} %param.34) | copy-start | bytes 73732
  166.3 3.7 %copy-start.4 = (bf16[4096,512]{1,0:T(8,128)(2,1)S(1)}, bf16[4096,512]{1,0:T(8,128)(2,1)}, u32[]{:S(2)}) copy-start(bf16[4096,512]{1,0:T(8,128)(2,1)} %param.30) | copy-start | bytes 12582916
  170.0 3.1 copy-start.10
  303.6 12.6 %copy-start.7 = (bf16[3,8,64,64]{3,2,1,0:T(8,128)(2,1)S(1)}, bf16[3,8,64,64]{3,2,1,0:T(8,128)(2,1)}, u32[]{:S(2)}) copy-start(bf16[3,8,64,64]{3,2,1,0:T(8,128)(2,1)} %copy-done.6) | copy-start | bytes 589828
  303.6 12.6 %copy-start.17 = (pred[8,2048]{1,0:T(8,128)(4,1)S(1)}, pred[8,2048]{1,0:T(8,128)(4,1)}, u32[]{:S(2)}) copy-start(pred[8,2048]{1,0:T(8,128)(4,1)} %iota_compare_fusion.1) | copy-start | bytes 49156
  337.9 18.3 %copy-start.1 = (bf16[256,2048]{1,0:T(8,128)(2,1)S(1)}, bf16[256,2048]{1,0:T(8,128)(2,1)}, u32[]{:S(2)}) copy-start(bf16[256,2048]{1,0:T(8,128)(2,1)} %param.19) | copy-start | bytes 3145732
  (2 other events, 2.5 us)
Sparse Core Ops, SparseCore 0:
  9.7 86.5 all-gather.5
  98.5 58.9 all-gather.3
  159.2 82.4 all-gather.7
where the time goes:
time: 364 us; the launch traced here: 363 us
  local copies, waits for them, and re-layouts  160 us (44%)
  matrix products  112 us (31%)
  other arithmetic  39.5 us (11%)
  starting transfers between devices  28.1 us (8%)
  between operations  14.7 us (4%)
  waiting for transfers between devices  8.41 us (2%)
    gather x1, local copies, waits for them, and re-layouts, on_device(): keys_latent = pool_latent[token_index]  71 us
    gather x1, local copies, waits for them, and re-layouts, on_device(): keys_rope = pool_rope[token_index]  57.8 us
    dot_general x4, matrix products, attend_group(): jnp.einsum('thl,hlv->thv', latent_out, value_map, preferred_element_type=...  30.8 us
    ppermute x8, starting transfers between devices, from_behind(): lax.ppermute(value, axis, [(source, source + steps) for source in range(f...  28 us
    sub x4, other arithmetic, masked_softmax(): raised = jnp.where(allowed, jnp.exp(scores - summit), 0.0)  20.3 us
    dot_general x4, matrix products, attend_group(): jnp.einsum('thl,jl->htj', query_part, window_latent, preferred_element_ty...  18.6 us
    unnamed x60, local copies, waits for them, and re-layouts  14 us
    dot_general x1, matrix products, decode_attend(): jnp.einsum('srhe,rke->srhk', query_rope, keys_rope, preferred_element_typ...  12.9 us
  transfers between devices with their start and end apart: 11, of which 2 were waited for; matrix products, arithmetic and copies ran while one was open for 84% of the time, Pallas kernels for 0%

commit v1 on v0

v1 whole, which is shorter than its diff:
```python
import jax
import jax.numpy as jnp
from jax import lax
from jax.experimental import pallas as pl
from jax.experimental.pallas import tpu as pltpu
from jax.sharding import PartitionSpec as P

DN, DR, DL, DV, PAGE = 128, 64, 512, 128, 64
F32, BF = jnp.float32, jnp.bfloat16
SCALE = (DN + DR) ** -0.5 * 1.4426950408889634
NEG = -1e30
KW = DL + 2 * DR
CHUNK = 768
MESH = pl.DeviceIdType.MESH


def nt(a, b):
    return lax.dot_general(a, b, (((1,), (1,)), ((), ())), preferred_element_type=F32)


def nn(a, b):
    return lax.dot_general(a, b, (((1,), (0,)), ((), ())), preferred_element_type=F32)


def half_lanes(pair, odd):
    lane = lax.broadcasted_iota(jnp.int32, pair.shape, 1)
    return jnp.where((lane >= DR) if odd else (lane < DR), pair, jnp.zeros_like(pair))


def kernel(
    lengths, hosts, pages, counts, row_slot,
    qn_h, qr_h, lat_h, rope_h, upk_h, upv_h, cl_h, cr_h, dq_h, dqr_h, nl_h, nr_h,
    pout_h, dout_h,
    allb, rope_st, pool, cr_st, upk, upv, qn, qr, pout, bias,
    qx, dqr, nl, nr, flip, qsend, qrecv, qrope, fresh, obuf, orecv, ysend, yrecv, dout,
    load_sem, z_send, z_recv, q_send, q_recv, o_send, o_recv, y_send, y_recv,
    a_send, a_recv, out_sem,
):
    z = lax.axis_index("dp")
    c = lax.axis_index("cp")
    core = lax.rem(c, 2)
    chip = lax.div(c, 2)
    cx, cy = lax.rem(chip, 4), lax.div(chip, 4)
    a = cx + core * (cy - cx)
    b = cy + core * (cx - cy)

    def at(da, db):
        pa, pb = lax.rem(a + da + 4, 4), lax.rem(b + db + 4, 4)
        return 2 * (pa * (1 + 3 * core) + pb * (4 - 3 * core)) + core

    sibling = c + 1 - 2 * core
    zp = [lax.rem(z + d, 4) for d in range(4)]

    loads = [
        (lat_h, allb.at[pl.ds(4 * c, 4), :, pl.ds(0, DL)]),
        (rope_h, rope_st),
        (dq_h.at[:, :, pl.ds(pl.multiple_of(z * 2048, 2048), 2048)], qx.at[z]),
        (upk_h, upk),
        (dqr_h, dqr),
        (nl_h, nl),
        (nr_h, nr),
        (cl_h, pool.at[:, :, pl.ds(0, DL)]),
        (cr_h, cr_st),
        (qn_h, qn),
        (qr_h, qr),
        (upv_h, upv),
    ]
    loads = [pltpu.make_async_copy(s, d, load_sem.at[i]) for i, (s, d) in enumerate(loads)]
    for one in loads:
        one.start()

    barrier = pltpu.get_barrier_semaphore()
    peers = [(z, at(1, 0)), (z, at(-1, 0)), (z, at(0, 1)), (z, at(0, -1)), (z, sibling)]
    peers += [(zp[d], c) for d in (1, 2, 3)]
    for peer in peers:
        pl.semaphore_signal(barrier, inc=1, device_id=peer, device_id_type=MESH)
    pl.semaphore_wait(barrier, len(peers))

    def remote(src, dst, send, recv, peer):
        return pltpu.make_async_remote_copy(
            src_ref=src, dst_ref=dst, send_sem=send, recv_sem=recv,
            device_id=peer, device_id_type=MESH)

    z_copies = []
    for d in (1, 2, 3):
        cols = pl.ds(pl.multiple_of(zp[d] * 2048, 2048), 2048)
        z_copies.append(remote(dq_h.at[:, :, cols], qx.at[z], z_send.at[d], z_recv.at[d], (zp[d], c)))
        z_copies[-1].start()

    loads[0].wait()
    loads[1].wait()
    own_rope = rope_st[...]
    allb[pl.ds(4 * c, 4), :, DL:] = jnp.concatenate([own_rope, own_rope], axis=2)

    def rows(block, half=None):
        if half is None:
            return allb.at[pl.ds(block * 4, 4)]
        return allb.at[pl.ds(block * 4 + half * 2, 2)]

    gather = {}
    slots = [0]

    def push(key, da, db, pa, pb, half=None):
        i = slots[0]
        slots[0] += 1
        ref = rows(at(da, db), half)
        copy = remote(ref, ref, a_send.at[i], a_recv.at[i], (z, at(pa, pb)))
        copy.start()
        gather[key] = copy

    def share(da, db):
        i = slots[0]
        slots[0] += 1
        ref = rows(at(da, db))
        copy = remote(ref, ref, a_send.at[i], a_recv.at[i], (z, sibling))
        copy.start()
        gather["s", da, db] = copy

    def got(*key):
        gather[key].wait_recv()

    push(("a", -1), 0, 0, 1, 0)
    push(("a", 1), 0, 0, -1, 0)
    push(("b", 0, -1), 0, 0, 0, 1)
    push(("b", 0, 1), 0, 0, 0, -1)
    share(0, 0)

    starts = [jnp.int32(0)]
    for r in range(7):
        starts.append(starts[-1] + lengths[r] * PAGE)
    query_pos = c * 256 + lax.broadcasted_iota(jnp.int32, (256, CHUNK), 0)
    low = jnp.zeros((256, CHUNK), jnp.int32)
    for r in range(1, 8):
        low = jnp.where(query_pos >= starts[r], starts[r], low)
    for part in range(3):
        key_pos = (c - 8) * 256 + part * CHUNK + lax.broadcasted_iota(jnp.int32, (256, CHUNK), 1)
        seen = (key_pos >= low) & (key_pos <= query_pos)
        bias[:, part * CHUNK:(part + 1) * CHUNK] = jnp.where(seen, 0.0, NEG)

    loads[4].wait()
    for owner in range(4):
        for pair in range(8):
            lanes = slice((owner * 8 + pair) * 128, (owner * 8 + pair + 1) * 128)
            value = jnp.concatenate([dqr[s, :, lanes].astype(F32) for s in range(3)], axis=0)
            for odd in range(2):
                flip[0, pl.ds(owner * 384 + pair * 2 + odd, 24, stride=16), :] = half_lanes(value, odd)
    for owner in range(4):
        qrope[owner] = flip[0, owner * 384:(owner + 1) * 384].reshape(24, 16, 128).astype(BF)

    loads[5].wait()
    loads[6].wait()
    for j in range(5):
        flip[j % 4, 0:128] = jnp.zeros((128, 128), F32)
        for s in range(3):
            if j < 4:
                value = nl[s, :, j * 128:(j + 1) * 128].astype(F32)
            else:
                value = nr[s].astype(F32)
                value = jnp.concatenate([value, value], axis=1)
            flip[j % 4, pl.ds(s, 8, stride=16), :] = value
        fresh[:, :, j * 128:(j + 1) * 128] = flip[j % 4, 0:128].reshape(8, 16, 128).astype(BF)

    loads[7].wait()
    loads[8].wait()
    old_rope = cr_st[...]
    pool[:, :, DL:] = jnp.concatenate([old_rope, old_rope], axis=2)

    loads[2].wait()
    loads[3].wait()
    for copy in z_copies:
        copy.wait_recv()

    def absorb(h, carry):
        lanes = pl.ds(pl.multiple_of(h * 128, 128), 128)
        value = jnp.concatenate(
            [qx[d, s, :, lanes].astype(F32) for d in range(4) for s in range(3)], axis=0)
        value = nn(value.astype(BF), upk[h])
        for j in range(4):
            flip[j, pl.ds(h, 96, stride=16), :] = value[:, j * 128:(j + 1) * 128]
        return carry

    lax.fori_loop(0, 16, absorb, 0)

    def spread(d, carry):
        for s in range(3):
            for i in range(8):
                base = pl.ds(pl.multiple_of((d * 24 + s * 8 + i) * 16, 16), 16)
                value = jnp.concatenate([flip[j, base, :] for j in range(4)], axis=1)
                qsend[d, (i // 2) * 6 + s * 2 + i % 2] = value.astype(BF)
        return carry

    lax.fori_loop(0, 4, spread, 0)

    q_copies = []
    for g in range(4):
        for d in (1, 2, 3):
            part = pl.ds(g * 6, 6)
            copy = remote(qsend.at[zp[d], part], qrecv.at[z, part],
                          q_send.at[d, g], q_recv.at[d, g], (zp[d], c))
            copy.start()
            q_copies.append(copy)
    q_own = pltpu.make_async_copy(qsend.at[z], qrecv.at[z], q_send.at[0, 0])
    q_own.start()

    got("a", -1)
    got("a", 1)
    push(("a2", 0), -1, 0, 1, 0, 0)
    push(("a2", 1), 1, 0, -1, 0, 1)
    for da in (-1, 1):
        push(("b", da, -1), da, 0, 0, 1)
        push(("b", da, 1), da, 0, 0, -1)
        share(da, 0)
    q_own.wait()

    row_step = lax.rem(lax.div(lax.broadcasted_iota(jnp.int32, (192, 16), 0), 16), 3)
    fresh_col = lax.broadcasted_iota(jnp.int32, (192, 16), 1)
    fresh_seen = (fresh_col <= row_step) & (fresh_col < 3)

    def attend(query, keys, used, recent):
        new = jnp.where(fresh_seen, nt(query, recent) * SCALE, NEG)
        scores = []
        top = jnp.max(new, axis=1, keepdims=True)
        for k in range(4):
            part = nt(query, keys(k)) * SCALE
            place = k * 512 + lax.broadcasted_iota(jnp.int32, (1, 512), 1)
            part = jnp.where(place < used, part, NEG)
            top = jnp.maximum(top, jnp.max(part, axis=1, keepdims=True))
            scores.append(part)
        new = jnp.exp2(new - top)
        total = jnp.sum(new, axis=1, keepdims=True)
        out = nn(new.astype(BF), recent[:, :DL])
        for k in range(4):
            part = jnp.exp2(scores[k] - top)
            total = total + jnp.sum(part, axis=1, keepdims=True)
            out = out + nn(part.astype(BF), keys(k)[:, :DL])
        return (out / total).astype(BF)

    def query_of(place, row):
        heads = [qrecv[o, place + 2 * s] for o in range(4) for s in range(3)]
        turns = [qrope[o, s * 8 + row] for o in range(4) for s in range(3)]
        return jnp.concatenate(
            [jnp.concatenate(heads, axis=0), jnp.concatenate(turns, axis=0)], axis=1)

    def decode_group(g):
        for e in range(2):
            row = 2 * g + e
            slot = row_slot[0, row]

            def keys(k):
                found = []
                for r in range(8):
                    page = jnp.minimum(pages[slot, k * 8 + r], 63)
                    found.append(pool[page])
                return jnp.concatenate(found, axis=0)

            out = attend(query_of(6 * g + e, row), keys, counts[slot], fresh[row])
            for o in range(4):
                for s in range(3):
                    obuf[o, 6 * g + 2 * s + e] = out[(o * 3 + s) * 16:(o * 3 + s + 1) * 16]

    o_copies = []

    def send_out(first, count, g):
        part = pl.ds(first, count)
        for d in (1, 2, 3):
            copy = remote(obuf.at[zp[d], part], orecv.at[z, part],
                          o_send.at[d, g], o_recv.at[d, g], (zp[d], c))
            copy.start()
            o_copies.append(copy)

    for g in range(4):
        for d in range(3):
            q_copies[g * 3 + d].wait_recv()
        decode_group(g)
        send_out(6 * g, 6, g)
        if g == 0:
            got("a2", 0)
            got("a2", 1)
            push(("b", 2, -1), 2, 0, 0, 1)
            push(("b", 2, 1), 2, 0, 0, -1)
            share(2, 0)
        if g == 1:
            for da in (0, -1, 1):
                got("b", da, -1)
                got("b", da, 1)
                push(("b2", da, 0), da, -1, 0, 1, 0)
                push(("b2", da, 1), da, 1, 0, -1, 1)
                share(da, -1)
                share(da, 1)
        if g == 2:
            got("b", 2, -1)
            got("b", 2, 1)
            push(("b2", 2, 0), 2, -1, 0, 1, 0)
            push(("b2", 2, 1), 2, 1, 0, -1, 1)
            share(2, -1)
            share(2, 1)
            for da in (0, -1, 1):
                got("b2", da, 0)
                got("b2", da, 1)
                share(da, 2)
        if g == 3:
            got("b2", 2, 0)
            got("b2", 2, 1)
            share(2, 2)
    for da in (0, -1, 1, 2):
        for db in (0, -1, 1, 2):
            got("s", da, db)

    device = z * 32 + c
    is_host = jnp.int32(0)
    arrival = jnp.int32(0)
    for r in range(8):
        hit = (hosts[r] == device).astype(jnp.int32)
        is_host = is_host + hit
        arrival = arrival + hit * lax.div(starts[r], PAGE)
    host_row = jnp.int32(0)
    for i in range(8):
        host_row = host_row + (row_slot[0, i] == 0).astype(jnp.int32) * i
    host_row = jnp.minimum(host_row, 7)

    def hosted_keys(k):
        found = []
        for r in range(8):
            page = jnp.minimum(arrival + k * 8 + r, 127)
            found.append(allb[page])
        return jnp.concatenate(found, axis=0)

    host_place = 6 * lax.div(host_row, 2) + lax.rem(host_row, 2)
    out = attend(query_of(host_place, host_row), hosted_keys, counts[0], fresh[host_row])
    for o in range(4):
        for s in range(3):
            obuf[o, 24 + s] = out[(o * 3 + s) * 16:(o * 3 + s + 1) * 16]
    send_out(24, 3, 4)

    loads[9].wait()
    loads[10].wait()
    loads[11].wait()

    def prefill_pair(p, carry):
        keys_up = upk[pl.ds(2 * p, 2)].reshape(256, DL)
        values_up = jnp.concatenate([upv[2 * p], upv[2 * p + 1]], axis=1)
        plain = qn[:, pl.ds(pl.multiple_of(p * 256, 256), 256)]
        turn = qr[:, pl.ds(pl.multiple_of(p * 128, 128), 128)]
        queries = [
            jnp.concatenate([plain[:, e * 128:(e + 1) * 128], half_lanes(turn, e)], axis=1)
            for e in range(2)
        ]
        state = [None, None]
        for part in (2, 1, 0):
            blocks = [lax.rem(c - 8 + part * 3 + i + 32, 32) for i in range(3)]
            rows_here = jnp.concatenate(
                [allb[pl.ds(block * 4, 4)].reshape(256, KW) for block in blocks], axis=0)
            latent = rows_here[:, :DL]
            head_keys = nt(latent, keys_up).astype(BF)
            head_values = nn(latent, values_up).astype(BF)
            shut = bias[:, part * CHUNK:(part + 1) * CHUNK]
            for e in range(2):
                key = jnp.concatenate([head_keys[:, e * 128:(e + 1) * 128], rows_here[:, DL:]], axis=1)
                value = jnp.concatenate(
                    [head_values[:, e * 128:(e + 1) * 128], jnp.ones((CHUNK, 128), BF)], axis=1)
                score = nt(queries[e], key) * SCALE + shut
                top = jnp.max(score, axis=1, keepdims=True)
                if state[e] is None:
                    weight = jnp.exp2(score - top)
                    total = nn(weight.astype(BF), value)
                else:
                    top = jnp.maximum(state[e][0], top)
                    weight = jnp.exp2(score - top)
                    total = state[e][1] * jnp.exp2(state[e][0] - top) + nn(weight.astype(BF), value)
                state[e] = (top, total)
        for e in range(2):
            total = state[e][1]
            pout[:, pl.ds(pl.multiple_of(p * 256 + e * 128, 128), 128)] = (
                total[:, :128] / total[:, 128:]).astype(BF)
        return carry

    lax.fori_loop(0, 8, prefill_pair, 0)
    pout_copy = pltpu.make_async_copy(pout, pout_h, out_sem.at[0])
    pout_copy.start()

    o_own = pltpu.make_async_copy(obuf.at[z, pl.ds(0, 27)], orecv.at[z, pl.ds(0, 27)], o_send.at[0, 0])
    o_own.start()
    for d in range(4):
        orecv[d, 27:32] = jnp.zeros((5, 16, DL), BF)
    for copy in o_copies:
        copy.wait_recv()
    o_own.wait()

    def unspread(t, carry):
        for u in range(8):
            value = orecv[lax.div(t, 4), lax.rem(t, 4) * 8 + u].astype(F32)
            base = pl.ds(pl.multiple_of((t * 8 + u) * 16, 16), 16)
            for j in range(4):
                flip[j, base, :] = value[:, j * 128:(j + 1) * 128]
        return carry

    lax.fori_loop(0, 16, unspread, 0)

    def project(h, carry):
        value = jnp.concatenate([flip[j, pl.ds(h, 128, stride=16), :] for j in range(4)], axis=1)
        value = nn(value.astype(BF), upv[h]).astype(BF)
        for d in range(4):
            ysend[d, :, pl.ds(pl.multiple_of(h * 128, 128), 128)] = value[d * 32:(d + 1) * 32]
        return carry

    lax.fori_loop(0, 16, project, 0)
    y_copies = []
    for d in (1, 2, 3):
        copy = remote(ysend.at[zp[d]], yrecv.at[z], y_send.at[d], y_recv.at[d], (zp[d], c))
        copy.start()
        y_copies.append(copy)
    y_own = pltpu.make_async_copy(ysend.at[z], yrecv.at[z], y_send.at[0])
    y_own.start()
    y_own.wait()
    for copy in y_copies:
        copy.wait_recv()

    row = lax.broadcasted_iota(jnp.int32, (8, 32), 0)
    place = lax.broadcasted_iota(jnp.int32, (8, 32), 1)
    for s in range(3):
        source = jnp.where((row == host_row) & (is_host > 0), 24 + s, lax.div(row, 2) * 6 + s * 2 + lax.rem(row, 2))
        pick = (place == source).astype(F32).astype(BF)
        for d in range(4):
            dout[s, :, d * 2048:(d + 1) * 2048] = nn(pick, yrecv[d]).astype(BF)
    dout_copy = pltpu.make_async_copy(dout, dout_h, out_sem.at[1])
    dout_copy.start()

    for copy in z_copies + q_copies + o_copies + y_copies + list(gather.values()):
        copy.wait_send()
    pout_copy.wait()
    dout_copy.wait()


def on_device(
    pre_q_nope, pre_q_rope, pre_latent, pre_rope, up_keys, up_values, new_lengths, new_hosts,
    req_pages, req_len, row_request, cache_latent, cache_rope, dec_q_nope, dec_q_rope,
    new_latent, new_rope,
):
    dma = pltpu.SemaphoreType.DMA
    vmem = pltpu.VMEM
    return pl.pallas_call(
        kernel,
        out_shape=(
            jax.ShapeDtypeStruct((256, 2048), BF),
            jax.ShapeDtypeStruct((3, 8, 8192), BF),
        ),
        in_specs=[pl.BlockSpec(memory_space=pltpu.SMEM)] * 5 + [pl.BlockSpec(memory_space=pl.ANY)] * 12,
        out_specs=[pl.BlockSpec(memory_space=pl.ANY)] * 2,
        scratch_shapes=[
            vmem((128, PAGE, KW), BF),
            vmem((4, PAGE, DR), BF),
            vmem((64, PAGE, KW), BF),
            vmem((64, PAGE, DR), BF),
            vmem((16, DN, DL), BF),
            vmem((16, DL, DV), BF),
            vmem((256, 2048), BF),
            vmem((256, 1024), BF),
            vmem((256, 2048), BF),
            vmem((256, 2304), F32),
            vmem((4, 3, 8, 2048), BF),
            vmem((3, 8, 4096), BF),
            vmem((3, 8, DL), BF),
            vmem((3, 8, DR), BF),
            vmem((4, 2048, 128), F32),
            vmem((4, 24, 16, DL), BF),
            vmem((4, 24, 16, DL), BF),
            vmem((4, 24, 16, 128), BF),
            vmem((8, 16, KW), BF),
            vmem((4, 32, 16, DL), BF),
            vmem((4, 32, 16, DL), BF),
            vmem((4, 32, 2048), BF),
            vmem((4, 32, 2048), BF),
            vmem((3, 8, 8192), BF),
            dma((12,)),
            dma((4,)), dma((4,)),
            dma((4, 4)), dma((4, 4)),
            dma((4, 5)), dma((4, 5)),
            dma((4,)), dma((4,)),
            dma((36,)), dma((36,)),
            dma((2,)),
        ],
        compiler_params=pltpu.CompilerParams(
            collective_id=0, has_side_effects=True, vmem_limit_bytes=60 * 2**20),
        cost_estimate=pl.CostEstimate(flops=25 * 10**9, bytes_accessed=16 * 2**20, transcendentals=12 * 10**6),
    )(
        new_lengths, new_hosts, req_pages, req_len, row_request,
        pre_q_nope, pre_q_rope, pre_latent.reshape(4, PAGE, DL), pre_rope.reshape(4, PAGE, DR), up_keys, up_values,
        cache_latent.reshape(64, PAGE, DL), cache_rope.reshape(64, PAGE, DR), dec_q_nope, dec_q_rope, new_latent, new_rope,
    )


def solution(mesh):
    placed = (
        P("cp", "dp"),
        P("cp", "dp"),
        P("cp", None),
        P("cp", None),
        P("dp", None, None),
        P("dp", None, None),
        P(),
        P(),
        P(("dp", "cp"), None),
        P(("dp", "cp")),
        P(("dp", "cp"), None),
        P(("dp", "cp"), None),
        P(("dp", "cp"), None),
        P(None, ("dp", "cp"), None),
        P(None, ("dp", "cp"), None),
        P(None, ("dp", "cp"), None),
        P(None, ("dp", "cp"), None),
    )
    return jax.shard_map(
        on_device,
        mesh=mesh,
        in_specs=placed,
        out_specs=(P("cp", "dp"), P(None, ("dp", "cp"), None)),
        check_vma=False,
    )
```

time: 364 us -> 97.9 us (0.27)
  local copies, waits for them, and re-layouts: 160 us -> 6.95 us
  matrix products: 112 us -> 0 us
  Pallas kernels: 0 us -> 90.1 us
  other arithmetic: 39.5 us -> 0 us
  starting transfers between devices: 28.1 us -> 0 us
  between operations: 14.7 us -> 0.65 us
  waiting for transfers between devices: 8.41 us -> 0 us
    gather x2 -> x0, local copies, waits for them, and re-layouts: 129 us -> none  [the longest x1 71 us: on_device(): keys_latent = pool_latent[token_index]]
    dot_general x20 -> x0, matrix products: 107 us -> none  [the longest x4 30.8 us: attend_group(): jnp.einsum('thl,hlv->thv', latent_out, value_map, preferred_element_type=...]
    pallas_call x0 -> x1, Pallas kernels: none -> 90.1 us  [on_device(): pl.pallas_call(kernel, out_shape=(jax.ShapeDtypeStruct((256, 2048), BF),...]
    ppermute x8 -> x0, starting transfers between devices: 28 us -> none  [from_behind(): lax.ppermute(value, axis, [(source, source + steps) for source in range(f...]
    sub x6 -> x0, other arithmetic: 20.9 us -> none  [the longest x4 20.3 us: masked_softmax(): raised = jnp.where(allowed, jnp.exp(scores - summit), 0.0)]
    reshape x4 -> x0, local copies, waits for them, and re-layouts: 11 us -> none  [the longest x1 7.43 us: on_device(): queries.reshape(token_rows, group_count, block_heads, DL)]
    reduce_sum x7 -> x0, other arithmetic: 8.24 us -> none  [the longest x1 6.38 us: decode_attend(): jnp.sum(cached_exp, axis=-1, keepdims=True)]
    ppermute x8 -> x0, waiting for transfers between devices: 7.66 us -> none  [from_behind(): lax.ppermute(value, axis, [(source, source + steps) for source in range(f...]
  transfers between devices with their start and end apart: 11 -> 0, of which waited for: 2 -> 0; matrix products, arithmetic and copies ran while one was open for 84% -> 0% of each run, Pallas kernels for 0% -> 0%
where the time goes in v1:
time: 97.9 us; the launch traced here: 97.7 us
  Pallas kernels  90.1 us (92%)
  local copies, waits for them, and re-layouts  6.95 us (7%)
    pallas_call x1, Pallas kernels, on_device(): pl.pallas_call(kernel, out_shape=(jax.ShapeDtypeStruct((256, 2048), BF),...  90.1 us
    unnamed x6, local copies, waits for them, and re-layouts  6.95 us

profile of v1, /device:TPU:1, one launch (start us, length us, event | category | flops | bytes accessed | tf_op | source)
XLA Modules:
  0.0 97.7 jit_solution(6522655780028434957)
XLA Ops:
  0.6 1.5 %copy.19 = bf16[256,64]{1,0:T(8,128)(2,1)} copy(bf16[256,64]{0,1:T(8,128)(2,1)} %param.20) | data formatting | bytes 65536 | tf_op args[3]
  2.1 2.4 %copy.20 = bf16[4096,64]{1,0:T(8,128)(2,1)} copy(bf16[4096,64]{0,1:T(8,128)(2,1)} %param.29) | data formatting | bytes 1048576 | tf_op args[12]
  4.5 90.1 %shard_map.176 = (bf16[256,2048]{1,0:T(8,128)(2,1)}, bf16[3,8,8192]{2,1,0:T(8,128)(2,1)}) custom-call(s32[8]{0:T(128)} %lengths.1, s32[8]{0:T(128)} %hosts.1, s32[8,32]{1,0:T(8,128)} %pages.1, s32[8]{0:T(128)} %counts.1, s32[1,8]{1,0:T(1,128)} %row_slot.1, bf16[256,2048]{1,0:T(8,128)(2,1)} %qn_h.1, bf16[256,1024]{1,0:T(8,128)(2,1)} %qr_h.1, ...), custom_call_target="tpu_custom_call" | custom-call | flops 24999999488 | bytes 16777216 | tf_op jit(solution)/shard_map/pallas_call | solution.py:441
  94.5 0.0 copy-start
  94.6 2.4 %copy.23 = bf16[256,2048]{1,0:T(8,128)(2,1)} copy(bf16[256,2048]{1,0:T(8,128)(2,1)} %get-tuple-element.4) | data formatting | bytes 2097152
  96.9 0.0 copy-done
  96.9 0.7 copy.24
Async XLA Ops:
  94.5 2.4 %copy-start = (bf16[3,8,8192]{2,1,0:T(8,128)(2,1)S(1)}, bf16[3,8,8192]{2,1,0:T(8,128)(2,1)}, u32[]{:S(2)}) copy-start(bf16[3,8,8192]{2,1,0:T(8,128)(2,1)} %get-tuple-element.5) | copy-start | bytes 1179652

commit v2 on v1

--- a/solution.py
+++ b/solution.py
@@ -32,9 +32,9 @@
     qn_h, qr_h, lat_h, rope_h, upk_h, upv_h, cl_h, cr_h, dq_h, dqr_h, nl_h, nr_h,
     pout_h, dout_h,
     allb, rope_st, pool, cr_st, upk, upv, qn, qr, pout, bias,
-    qx, dqr, nl, nr, flip, qsend, qrecv, qrope, fresh, obuf, orecv, ysend, yrecv, dout,
+    qx, dqr, nl, nr, tops, totals, flip, qsend, qrecv, qrope, fresh, obuf, orecv, ysend, yrecv, dout,
     load_sem, z_send, z_recv, q_send, q_recv, o_send, o_recv, y_send, y_recv,
-    a_send, a_recv, out_sem,
+    a_send, a_recv, near_send, near_recv, out_sem,
 ):
     z = lax.axis_index("dp")
     c = lax.axis_index("cp")
@@ -71,7 +71,8 @@
 
     barrier = pltpu.get_barrier_semaphore()
     peers = [(z, at(1, 0)), (z, at(-1, 0)), (z, at(0, 1)), (z, at(0, -1)), (z, sibling)]
-    peers += [(zp[d], c) for d in (1, 2, 3)]
+    after, before = lax.rem(c + 2, 32), lax.rem(c + 30, 32)
+    peers += [(zp[d], c) for d in (1, 2, 3)] + [(z, after), (z, before)]
     for peer in peers:
         pl.semaphore_signal(barrier, inc=1, device_id=peer, device_id_type=MESH)
     pl.semaphore_wait(barrier, len(peers))
@@ -89,13 +90,22 @@
 
     loads[0].wait()
     loads[1].wait()
-    own_rope = rope_st[...]
-    allb[pl.ds(4 * c, 4), :, DL:] = jnp.concatenate([own_rope, own_rope], axis=2)
+    own_rope = rope_st[...].astype(F32)
+    own_rope = jnp.concatenate([own_rope, own_rope], axis=0).T
+    allb[pl.ds(4 * c, 4), :, DL:] = own_rope.reshape(4, PAGE, 128).astype(BF)
 
     def rows(block, half=None):
         if half is None:
             return allb.at[pl.ds(block * 4, 4)]
         return allb.at[pl.ds(block * 4 + half * 2, 2)]
+
+    near = [
+        remote(rows(c), rows(32), near_send.at[0], near_recv.at[0], (z, after)),
+        remote(rows(c), rows(33), near_send.at[1], near_recv.at[1], (z, sibling)),
+        remote(rows(32), rows(34), near_send.at[2], near_recv.at[2], (z, sibling)),
+    ]
+    near[0].start()
+    near[1].start()
 
     gather = {}
     slots = [0]
@@ -162,8 +172,13 @@
 
     loads[7].wait()
     loads[8].wait()
-    old_rope = cr_st[...]
-    pool[:, :, DL:] = jnp.concatenate([old_rope, old_rope], axis=2)
+    for i in range(8):
+        old_rope = cr_st[:, i * 512:(i + 1) * 512].astype(F32)
+        old_rope = jnp.concatenate([old_rope, old_rope], axis=0).T
+        pool[i * 8:(i + 1) * 8, :, DL:] = old_rope.reshape(8, PAGE, 128).astype(BF)
+
+    near[0].wait_recv()
+    near[2].start()
 
     loads[2].wait()
     loads[3].wait()
@@ -179,7 +194,7 @@
             flip[j, pl.ds(h, 96, stride=16), :] = value[:, j * 128:(j + 1) * 128]
         return carry
 
-    lax.fori_loop(0, 16, absorb, 0)
+    lax.fori_loop(0, 16, absorb, 0, unroll=4)
 
     def spread(d, carry):
         for s in range(3):
@@ -212,28 +227,108 @@
         share(da, 0)
     q_own.wait()
 
+    def prefill_part(p, part, state):
+        keys_up = upk[pl.ds(2 * p, 2)].reshape(256, DL)
+        values_up = jnp.concatenate([upv[2 * p], upv[2 * p + 1]], axis=1)
+        plain = qn[:, pl.ds(pl.multiple_of(p * 256, 256), 256)]
+        turn = qr[:, pl.ds(pl.multiple_of(p * 128, 128), 128)]
+        if part == 2:
+            blocks = [32, 34 - core, c]
+        else:
+            blocks = [lax.rem(c - 8 + part * 3 + i + 32, 32) for i in range(3)]
+        rows_here = jnp.concatenate(
+            [allb[pl.ds(block * 4, 4)].reshape(256, KW) for block in blocks], axis=0)
+        latent = rows_here[:, :DL]
+        head_keys = nt(latent, keys_up).astype(BF)
+        head_values = nn(latent, values_up).astype(BF)
+        shut = bias[:, part * CHUNK:(part + 1) * CHUNK]
+        following = []
+        for e in range(2):
+            query = jnp.concatenate([plain[:, e * 128:(e + 1) * 128], half_lanes(turn, e)], axis=1)
+            key = jnp.concatenate([head_keys[:, e * 128:(e + 1) * 128], rows_here[:, DL:]], axis=1)
+            value = jnp.concatenate(
+                [head_values[:, e * 128:(e + 1) * 128], jnp.ones((CHUNK, 128), BF)], axis=1)
+            score = nt(query, key) * SCALE + shut
+            top = jnp.max(score, axis=1, keepdims=True)
+            if state is None:
+                weight = jnp.exp2(score - top)
+                total = nn(weight.astype(BF), value)
+            else:
+                old_top, old_total = state[e]
+                top = jnp.maximum(old_top, top)
+                weight = jnp.exp2(score - top)
+                total = old_total * jnp.exp2(old_top - top) + nn(weight.astype(BF), value)
+            following.append((top, total))
+        return following
+
+    def prefill_near(p, carry):
+        for e, (top, total) in enumerate(prefill_part(p, 2, None)):
+            lane = lax.broadcasted_iota(jnp.int32, (256, 128), 1)
+            tops[2 * p + e] = jnp.where(lane < 64, top, total[:, 128:])
+            totals[2 * p + e] = total[:, :128]
+        return carry
+
+    def prefill_far(p, carry):
+        state = []
+        for e in range(2):
+            known = tops[2 * p + e]
+            summed = jnp.broadcast_to(known[:, 64:65], (256, 128))
+            state.append((known[:, :1], jnp.concatenate([totals[2 * p + e], summed], axis=1)))
+        for part in (1, 0):
+            state = prefill_part(p, part, state)
+        for e in range(2):
+            total = state[e][1]
+            pout[:, pl.ds(pl.multiple_of(p * 256 + e * 128, 128), 128)] = (
+                total[:, :128] / total[:, 128:]).astype(BF)
+        return carry
+
+    near[1].wait_recv()
+    near[2].wait_recv()
+    loads[9].wait()
+    loads[10].wait()
+    loads[11].wait()
+    lax.fori_loop(0, 4, prefill_near, 0, unroll=2)
+    got("a2", 0)
+    got("a2", 1)
+    push(("b", 2, -1), 2, 0, 0, 1)
+    push(("b", 2, 1), 2, 0, 0, -1)
+    share(2, 0)
+    got("b", 0, -1)
+    got("b", 0, 1)
+    push(("b2", 0, 0), 0, -1, 0, 1, 0)
+    push(("b2", 0, 1), 0, 1, 0, -1, 1)
+    share(0, -1)
+    share(0, 1)
+    lax.fori_loop(4, 8, prefill_near, 0, unroll=2)
+
     row_step = lax.rem(lax.div(lax.broadcasted_iota(jnp.int32, (192, 16), 0), 16), 3)
     fresh_col = lax.broadcasted_iota(jnp.int32, (192, 16), 1)
     fresh_seen = (fresh_col <= row_step) & (fresh_col < 3)
 
-    def attend(query, keys, used, recent):
-        new = jnp.where(fresh_seen, nt(query, recent) * SCALE, NEG)
-        scores = []
-        top = jnp.max(new, axis=1, keepdims=True)
+    def attend(queries, keys, used, recent):
+        count = len(queries)
+        new, scores, top = [], [[] for _ in range(count)], []
+        for e in range(count):
+            new.append(jnp.where(fresh_seen, nt(queries[e], recent[e]) * SCALE, NEG))
+            top.append(jnp.max(new[e], axis=1, keepdims=True))
         for k in range(4):
-            part = nt(query, keys(k)) * SCALE
             place = k * 512 + lax.broadcasted_iota(jnp.int32, (1, 512), 1)
-            part = jnp.where(place < used, part, NEG)
-            top = jnp.maximum(top, jnp.max(part, axis=1, keepdims=True))
-            scores.append(part)
-        new = jnp.exp2(new - top)
-        total = jnp.sum(new, axis=1, keepdims=True)
-        out = nn(new.astype(BF), recent[:, :DL])
+            for e in range(count):
+                part = nt(queries[e], keys(e, k)) * SCALE
+                part = jnp.where(place < used[e], part, NEG)
+                top[e] = jnp.maximum(top[e], jnp.max(part, axis=1, keepdims=True))
+                scores[e].append(part)
+        total, out = [], []
+        for e in range(count):
+            fresh_weight = jnp.exp2(new[e] - top[e])
+            total.append(jnp.sum(fresh_weight, axis=1, keepdims=True))
+            out.append(nn(fresh_weight.astype(BF), recent[e][:, :DL]))
         for k in range(4):
-            part = jnp.exp2(scores[k] - top)
-            total = total + jnp.sum(part, axis=1, keepdims=True)
-            out = out + nn(part.astype(BF), keys(k)[:, :DL])
-        return (out / total).astype(BF)
+            for e in range(count):
+                part = jnp.exp2(scores[e][k] - top[e])
+                total[e] = total[e] + jnp.sum(part, axis=1, keepdims=True)
+                out[e] = out[e] + nn(part.astype(BF), keys(e, k)[:, :DL])
+        return [(out[e] / total[e]).astype(BF) for e in range(count)]
 
     def query_of(place, row):
         heads = [qrecv[o, place + 2 * s] for o in range(4) for s in range(3)]
@@ -242,21 +337,22 @@
             [jnp.concatenate(heads, axis=0), jnp.concatenate(turns, axis=0)], axis=1)
 
     def decode_group(g):
+        slots_here = [row_slot[0, 2 * g + e] for e in range(2)]
+
+        def keys(e, k):
+            found = []
+            for r in range(8):
+                page = jnp.minimum(pages[slots_here[e], k * 8 + r], 63)
+                found.append(pool[page])
+            return jnp.concatenate(found, axis=0)
+
+        outs = attend(
+            [query_of(6 * g + e, 2 * g + e) for e in range(2)], keys,
+            [counts[slot] for slot in slots_here], [fresh[2 * g + e] for e in range(2)])
         for e in range(2):
-            row = 2 * g + e
-            slot = row_slot[0, row]
-
-            def keys(k):
-                found = []
-                for r in range(8):
-                    page = jnp.minimum(pages[slot, k * 8 + r], 63)
-                    found.append(pool[page])
-                return jnp.concatenate(found, axis=0)
-
-            out = attend(query_of(6 * g + e, row), keys, counts[slot], fresh[row])
             for o in range(4):
                 for s in range(3):
-                    obuf[o, 6 * g + 2 * s + e] = out[(o * 3 + s) * 16:(o * 3 + s + 1) * 16]
+                    obuf[o, 6 * g + 2 * s + e] = outs[e][(o * 3 + s) * 16:(o * 3 + s + 1) * 16]
 
     o_copies = []
 
@@ -274,27 +370,25 @@
         decode_group(g)
         send_out(6 * g, 6, g)
         if g == 0:
-            got("a2", 0)
-            got("a2", 1)
-            push(("b", 2, -1), 2, 0, 0, 1)
-            push(("b", 2, 1), 2, 0, 0, -1)
-            share(2, 0)
-        if g == 1:
-            for da in (0, -1, 1):
+            for da in (-1, 1):
                 got("b", da, -1)
                 got("b", da, 1)
                 push(("b2", da, 0), da, -1, 0, 1, 0)
                 push(("b2", da, 1), da, 1, 0, -1, 1)
                 share(da, -1)
                 share(da, 1)
-        if g == 2:
+        if g == 1:
             got("b", 2, -1)
             got("b", 2, 1)
             push(("b2", 2, 0), 2, -1, 0, 1, 0)
             push(("b2", 2, 1), 2, 1, 0, -1, 1)
             share(2, -1)
             share(2, 1)
-            for da in (0, -1, 1):
+            got("b2", 0, 0)
+            got("b2", 0, 1)
+            share(0, 2)
+        if g == 2:
+            for da in (-1, 1):
                 got("b2", da, 0)
                 got("b2", da, 1)
                 share(da, 2)
@@ -318,7 +412,7 @@
         host_row = host_row + (row_slot[0, i] == 0).astype(jnp.int32) * i
     host_row = jnp.minimum(host_row, 7)
 
-    def hosted_keys(k):
+    def hosted_keys(e, k):
         found = []
         for r in range(8):
             page = jnp.minimum(arrival + k * 8 + r, 127)
@@ -326,57 +420,17 @@
         return jnp.concatenate(found, axis=0)
 
     host_place = 6 * lax.div(host_row, 2) + lax.rem(host_row, 2)
-    out = attend(query_of(host_place, host_row), hosted_keys, counts[0], fresh[host_row])
+    out = attend([query_of(host_place, host_row)], hosted_keys, [counts[0]], [fresh[host_row]])[0]
     for o in range(4):
         for s in range(3):
             obuf[o, 24 + s] = out[(o * 3 + s) * 16:(o * 3 + s + 1) * 16]
     send_out(24, 3, 4)
 
-    loads[9].wait()
-    loads[10].wait()
-    loads[11].wait()
-
-    def prefill_pair(p, carry):
-        keys_up = upk[pl.ds(2 * p, 2)].reshape(256, DL)
-        values_up = jnp.concatenate([upv[2 * p], upv[2 * p + 1]], axis=1)
-        plain = qn[:, pl.ds(pl.multiple_of(p * 256, 256), 256)]
-        turn = qr[:, pl.ds(pl.multiple_of(p * 128, 128), 128)]
-        queries = [
-            jnp.concatenate([plain[:, e * 128:(e + 1) * 128], half_lanes(turn, e)], axis=1)
-            for e in range(2)
-        ]
-        state = [None, None]
-        for part in (2, 1, 0):
-            blocks = [lax.rem(c - 8 + part * 3 + i + 32, 32) for i in range(3)]
-            rows_here = jnp.concatenate(
-                [allb[pl.ds(block * 4, 4)].reshape(256, KW) for block in blocks], axis=0)
-            latent = rows_here[:, :DL]
-            head_keys = nt(latent, keys_up).astype(BF)
-            head_values = nn(latent, values_up).astype(BF)
-            shut = bias[:, part * CHUNK:(part + 1) * CHUNK]
-            for e in range(2):
-                key = jnp.concatenate([head_keys[:, e * 128:(e + 1) * 128], rows_here[:, DL:]], axis=1)
-                value = jnp.concatenate(
-                    [head_values[:, e * 128:(e + 1) * 128], jnp.ones((CHUNK, 128), BF)], axis=1)
-                score = nt(queries[e], key) * SCALE + shut
-                top = jnp.max(score, axis=1, keepdims=True)
-                if state[e] is None:
-                    weight = jnp.exp2(score - top)
-                    total = nn(weight.astype(BF), value)
-                else:
-                    top = jnp.maximum(state[e][0], top)
-                    weight = jnp.exp2(score - top)
-                    total = state[e][1] * jnp.exp2(state[e][0] - top) + nn(weight.astype(BF), value)
-                state[e] = (top, total)
-        for e in range(2):
-            total = state[e][1]
-            pout[:, pl.ds(pl.multiple_of(p * 256 + e * 128, 128), 128)] = (
-                total[:, :128] / total[:, 128:]).astype(BF)
-        return carry
-
-    lax.fori_loop(0, 8, prefill_pair, 0)
-    pout_copy = pltpu.make_async_copy(pout, pout_h, out_sem.at[0])
-    pout_copy.start()
+    early = 6
+    lax.fori_loop(0, early, prefill_far, 0, unroll=2)
+    pout_copies = [
+        pltpu.make_async_copy(pout.at[:, pl.ds(0, early * 256)], pout_h.at[:, pl.ds(0, early * 256)], out_sem.at[0])]
+    pout_copies[0].start()
 
     o_own = pltpu.make_async_copy(obuf.at[z, pl.ds(0, 27)], orecv.at[z, pl.ds(0, 27)], o_send.at[0, 0])
     o_own.start()
@@ -403,7 +457,7 @@
             ysend[d, :, pl.ds(pl.multiple_of(h * 128, 128), 128)] = value[d * 32:(d + 1) * 32]
         return carry
 
-    lax.fori_loop(0, 16, project, 0)
+    lax.fori_loop(0, 16, project, 0, unroll=4)
     y_copies = []
     for d in (1, 2, 3):
         copy = remote(ysend.at[zp[d]], yrecv.at[z], y_send.at[d], y_recv.at[d], (zp[d], c))
@@ -411,6 +465,11 @@
         y_copies.append(copy)
     y_own = pltpu.make_async_copy(ysend.at[z], yrecv.at[z], y_send.at[0])
     y_own.start()
+
+    lax.fori_loop(early, 8, prefill_far, 0, unroll=2)
+    late = pl.ds(early * 256, 2048 - early * 256)
+    pout_copies.append(pltpu.make_async_copy(pout.at[:, late], pout_h.at[:, late], out_sem.at[2]))
+    pout_copies[1].start()
     y_own.wait()
     for copy in y_copies:
         copy.wait_recv()
@@ -427,7 +486,10 @@
 
     for copy in z_copies + q_copies + o_copies + y_copies + list(gather.values()):
         copy.wait_send()
-    pout_copy.wait()
+    for copy in near:
+        copy.wait_send()
+    for copy in pout_copies:
+        copy.wait()
     dout_copy.wait()
 
 
@@ -447,10 +509,10 @@
         in_specs=[pl.BlockSpec(memory_space=pltpu.SMEM)] * 5 + [pl.BlockSpec(memory_space=pl.ANY)] * 12,
         out_specs=[pl.BlockSpec(memory_space=pl.ANY)] * 2,
         scratch_shapes=[
-            vmem((128, PAGE, KW), BF),
-            vmem((4, PAGE, DR), BF),
+            vmem((140, PAGE, KW), BF),
+            vmem((DR, 256), BF),
             vmem((64, PAGE, KW), BF),
-            vmem((64, PAGE, DR), BF),
+            vmem((DR, 4096), BF),
             vmem((16, DN, DL), BF),
             vmem((16, DL, DV), BF),
             vmem((256, 2048), BF),
@@ -461,6 +523,8 @@
             vmem((3, 8, 4096), BF),
             vmem((3, 8, DL), BF),
             vmem((3, 8, DR), BF),
+            vmem((16, 256, 128), F32),
+            vmem((16, 256, 128), F32),
             vmem((4, 2048, 128), F32),
             vmem((4, 24, 16, DL), BF),
             vmem((4, 24, 16, DL), BF),
@@ -477,15 +541,16 @@
             dma((4, 5)), dma((4, 5)),
             dma((4,)), dma((4,)),
             dma((36,)), dma((36,)),
-            dma((2,)),
+            dma((3,)), dma((3,)),
+            dma((3,)),
         ],
         compiler_params=pltpu.CompilerParams(
             collective_id=0, has_side_effects=True, vmem_limit_bytes=60 * 2**20),
         cost_estimate=pl.CostEstimate(flops=25 * 10**9, bytes_accessed=16 * 2**20, transcendentals=12 * 10**6),
     )(
         new_lengths, new_hosts, req_pages, req_len, row_request,
-        pre_q_nope, pre_q_rope, pre_latent.reshape(4, PAGE, DL), pre_rope.reshape(4, PAGE, DR), up_keys, up_values,
-        cache_latent.reshape(64, PAGE, DL), cache_rope.reshape(64, PAGE, DR), dec_q_nope, dec_q_rope, new_latent, new_rope,
+        pre_q_nope, pre_q_rope, pre_latent.reshape(4, PAGE, DL), pre_rope.T, up_keys, up_values,
+        cache_latent.reshape(64, PAGE, DL), cache_rope.T, dec_q_nope, dec_q_rope, new_latent, new_rope,
     )
 
 

time: 97.9 us -> 83.1 us (0.85)
  Pallas kernels: 90.1 us -> 79.2 us
  local copies, waits for them, and re-layouts: 6.95 us -> 3.1 us
    pallas_call x1, Pallas kernels: 90.1 us -> 79.2 us  [on_device(): pl.pallas_call(kernel, out_shape=(jax.ShapeDtypeStruct((256, 2048), BF),...]
    unnamed x6 -> x4, local copies, waits for them, and re-layouts: 6.95 us -> 3.1 us
where the time goes in v2:
time: 83.1 us; the launch traced here: 83 us
  Pallas kernels  79.2 us (95%)
  local copies, waits for them, and re-layouts  3.1 us (4%)
    pallas_call x1, Pallas kernels, on_device(): pl.pallas_call(kernel, out_shape=(jax.ShapeDtypeStruct((256, 2048), BF),...  79.2 us
    unnamed x4, local copies, waits for them, and re-layouts  3.1 us

profile of v2, /device:TPU:1, one launch (start us, length us, event | category | flops | bytes accessed | tf_op | source)
XLA Modules:
  0.0 83.0 jit_solution(14737034979489549778)
XLA Ops:
  0.6 79.2 %shard_map.176 = (bf16[256,2048]{1,0:T(8,128)(2,1)}, bf16[3,8,8192]{2,1,0:T(8,128)(2,1)}) custom-call(s32[8]{0:T(128)} %lengths.1, s32[8]{0:T(128)} %hosts.1, s32[8,32]{1,0:T(8,128)} %pages.1, s32[8]{0:T(128)} %counts.1, s32[1,8]{1,0:T(1,128)} %row_slot.1, bf16[256,2048]{1,0:T(8,128)(2,1)} %qn_h.1, bf16[256,1024]{1,0:T(8,128)(2,1)} %qr_h.1, ...), custom_call_target="tpu_custom_call" | custom-call | flops 24999999488 | bytes 16777216 | tf_op jit(solution)/shard_map/pallas_call | solution.py:503
  79.8 0.0 copy-start
  79.8 2.4 %copy.21 = bf16[256,2048]{1,0:T(8,128)(2,1)} copy(bf16[256,2048]{1,0:T(8,128)(2,1)} %get-tuple-element.4) | data formatting | bytes 2097152
  82.2 0.0 copy-done
  82.2 0.7 copy.22
Async XLA Ops:
  79.8 2.4 %copy-start = (bf16[3,8,8192]{2,1,0:T(8,128)(2,1)S(1)}, bf16[3,8,8192]{2,1,0:T(8,128)(2,1)}, u32[]{:S(2)}) copy-start(bf16[3,8,8192]{2,1,0:T(8,128)(2,1)} %get-tuple-element.5) | copy-start | bytes 1179652

commit v3 on v2

--- a/solution.py
+++ b/solution.py
@@ -388,17 +388,21 @@
             got("b2", 0, 1)
             share(0, 2)
         if g == 2:
-            for da in (-1, 1):
-                got("b2", da, 0)
-                got("b2", da, 1)
-                share(da, 2)
-        if g == 3:
-            got("b2", 2, 0)
-            got("b2", 2, 1)
-            share(2, 2)
+            got("b2", -1, 0)
+            got("b2", -1, 1)
+            share(-1, 2)
+    later = ((1, 2), (2, 2))
     for da in (0, -1, 1, 2):
         for db in (0, -1, 1, 2):
-            got("s", da, db)
+            if (da, db) not in later:
+                got("s", da, db)
+    lax.fori_loop(0, 4, prefill_far, 0, unroll=2)
+    for da, db in later:
+        got("b2", da, 0)
+        got("b2", da, 1)
+        share(da, db)
+    for key in later:
+        got("s", *key)
 
     device = z * 32 + c
     is_host = jnp.int32(0)
@@ -427,7 +431,7 @@
     send_out(24, 3, 4)
 
     early = 6
-    lax.fori_loop(0, early, prefill_far, 0, unroll=2)
+    lax.fori_loop(4, early, prefill_far, 0, unroll=2)
     pout_copies = [
         pltpu.make_async_copy(pout.at[:, pl.ds(0, early * 256)], pout_h.at[:, pl.ds(0, early * 256)], out_sem.at[0])]
     pout_copies[0].start()

time: 83.1 us -> 82.7 us (level)
  no operation moved by 1% of the time
where the time goes in v3:
time: 82.7 us; the launch traced here: 82.5 us
  Pallas kernels  78.8 us (95%)
  local copies, waits for them, and re-layouts  3.1 us (4%)
    pallas_call x1, Pallas kernels, on_device(): pl.pallas_call(kernel, out_shape=(jax.ShapeDtypeStruct((256, 2048), BF),...  78.8 us
    unnamed x4, local copies, waits for them, and re-layouts  3.1 us

profile of v3, /device:TPU:1, one launch (start us, length us, event | category | flops | bytes accessed | tf_op | source)
XLA Modules:
  0.0 82.5 jit_solution(9223045454881438720)
XLA Ops:
  0.6 78.8 %shard_map.176 = (bf16[256,2048]{1,0:T(8,128)(2,1)}, bf16[3,8,8192]{2,1,0:T(8,128)(2,1)}) custom-call(s32[8]{0:T(128)} %lengths.1, s32[8]{0:T(128)} %hosts.1, s32[8,32]{1,0:T(8,128)} %pages.1, s32[8]{0:T(128)} %counts.1, s32[1,8]{1,0:T(1,128)} %row_slot.1, bf16[256,2048]{1,0:T(8,128)(2,1)} %qn_h.1, bf16[256,1024]{1,0:T(8,128)(2,1)} %qr_h.1, ...), custom_call_target="tpu_custom_call" | custom-call | flops 24999999488 | bytes 16777216 | tf_op jit(solution)/shard_map/pallas_call | solution.py:507
  79.4 0.0 copy-start
  79.4 2.4 %copy.21 = bf16[256,2048]{1,0:T(8,128)(2,1)} copy(bf16[256,2048]{1,0:T(8,128)(2,1)} %get-tuple-element.4) | data formatting | bytes 2097152
  81.8 0.0 copy-done
  81.8 0.7 copy.22
Async XLA Ops:
  79.4 2.4 %copy-start = (bf16[3,8,8192]{2,1,0:T(8,128)(2,1)S(1)}, bf16[3,8,8192]{2,1,0:T(8,128)(2,1)}, u32[]{:S(2)}) copy-start(bf16[3,8,8192]{2,1,0:T(8,128)(2,1)} %get-tuple-element.5) | copy-start | bytes 1179652
